TPU v7x, 32 devices: a whole 2x2x4 slice. The times are simulated.
32 devices in a mesh: samp: 8 (over z, x), blk: 4 (over y, core).
Axes of the slice: x: 2, y: 2, z: 4, core: 2. Of those that a mesh axis runs over, the one named last changes fastest.
Arguments:
- dosages: int32 [12288, 2048], P('samp', 'blk'), may hold values from 0 to 2, as said below
- new_dosages: int32 [12288, 512], P('samp', 'blk'), may hold values from 0 to 2, as said below
- traits: float32 [64, 12288], P(None, 'samp'), may hold values from -40 to 40
- shrink: float32 [5], replicated, may hold values from 0.5 to 5
Outputs:
- residual: float32 [5, 64, 12288], P(None, 'blk', 'samp')
- scores: float32 [5, 64, 512], P(None, None, 'blk')
Inputs may be any that keep to these rules, and one draw needn't show every extreme that they name: `dosages`: codes of haplotype pairs, with linkage along neighbouring variants. `new_dosages`: codes of haplotype pairs, with linkage along neighbouring variants.
All inputs are finite; a program needn't handle non-finite values.
Results may differ from a plain program's by a relative error of at most 0.0053.
Values may be sent and summed in bfloat16 or wider, within the bound.
A program may use at most 64 MiB of HBM per device.

v0:
```python
import jax
import jax.numpy as jnp
from jax import lax
from jax.sharding import PartitionSpec as P

RIDGE = 5
CHEB = 3


def chebyshev(rhs_cols, apply_fn, centre, half_width, sweeps):
    sig_ratio = centre / half_width
    factor = 1.0 / sig_ratio
    direction = rhs_cols / centre
    iterate = jnp.zeros_like(rhs_cols)
    remain = rhs_cols
    for sweep_index in range(sweeps):
        iterate = iterate + direction
        if sweep_index + 1 < sweeps:
            remain = remain - apply_fn(direction)
            factor_next = 1.0 / (2.0 * sig_ratio - factor)
            direction = factor_next * factor * direction + 2.0 * factor_next / half_width * remain
            factor = factor_next
    return iterate


def scaled(values, column_sum, column_sq, count):
    column_mean = column_sum / count
    column_var = column_sq / count - column_mean * column_mean
    inverse = 1.0 / jnp.sqrt(column_var + 1e-05)
    return ((values - column_mean) * inverse).astype(jnp.bfloat16)


def shards(dosages, new_dosages, traits, shrink):
    local_rows = dosages.shape[0]
    trait_count = traits.shape[0]
    count = float(local_rows * lax.axis_size("samp"))
    block_codes = dosages.astype(jnp.float32)
    new_codes = new_dosages.astype(jnp.float32)
    block_sum, block_sq, new_sum, new_sq = lax.psum(
        (
            jnp.sum(block_codes, axis=0),
            jnp.sum(block_codes * block_codes, axis=0),
            jnp.sum(new_codes, axis=0),
            jnp.sum(new_codes * new_codes, axis=0),
        ),
        "samp",
    )
    standard = scaled(block_codes, block_sum, block_sq, count)
    fresh = scaled(new_codes, new_sum, new_sq, count)
    trait_bf = traits.astype(jnp.bfloat16)
    gram = lax.dot_general(
        standard, standard, (((0,), (0,)), ((), ())), preferred_element_type=jnp.float32
    )
    cross = lax.dot_general(
        standard, trait_bf, (((0,), (1,)), ((), ())), preferred_element_type=jnp.float32
    )
    lam_cols = jnp.repeat(shrink, trait_count)
    gram_full, cross_full = lax.psum((gram, cross), "samp")
    bound = jnp.max(jnp.sum(jnp.abs(gram_full), axis=0)) / count

    def apply_full(direction):
        return (
            jnp.dot(gram_full, direction, precision=lax.Precision.HIGHEST) / count
            + lam_cols * direction
        )

    rhs_cols = jnp.tile(cross_full / count, (1, RIDGE))
    weights = chebyshev(
        rhs_cols, apply_full, lam_cols + bound / 2.0, bound / 2.0 + jnp.zeros_like(lam_cols), CHEB
    )
    weight_bf = weights.astype(jnp.bfloat16)
    pred = lax.dot_general(
        weight_bf, standard, (((0,), (1,)), ((), ())), preferred_element_type=jnp.float32
    )
    pred = pred.reshape(RIDGE, trait_count, local_rows)
    share = trait_count // lax.axis_size("blk")
    pred_part = lax.psum_scatter(pred, "blk", scatter_dimension=1, tiled=True)
    own_traits = lax.dynamic_slice_in_dim(traits, lax.axis_index("blk") * share, share, 0)
    residual = own_traits[None, :, :] - pred_part
    res_bf = lax.all_gather(residual.astype(jnp.bfloat16), "blk", axis=1, tiled=True)
    res_flat = res_bf.reshape(RIDGE * trait_count, local_rows)
    raw_part = jnp.dot(res_flat, fresh, preferred_element_type=jnp.float32)
    res_float = res_flat.astype(jnp.float32)
    raw, sum_sq = lax.psum((raw_part, jnp.sum(res_float * res_float, axis=1)), "samp")
    scores = raw / jnp.sqrt(count * (sum_sq / count + 1e-05))[:, None]
    return (residual, scores.reshape(RIDGE, trait_count, fresh.shape[1]))


def solution(mesh):
    placed = (P("samp", "blk"), P("samp", "blk"), P(None, "samp"), P())
    return jax.shard_map(
        shards,
        mesh=mesh,
        in_specs=placed,
        out_specs=(P(None, "blk", "samp"), P(None, None, "blk")),
        check_vma=False,
    )
```

profile of v0, /device:TPU:1, one launch (start us, length us, event | category | flops | bytes accessed | tf_op | source)
XLA Modules:
  0.0 260.9 jit_solution(1093305931093458666)
XLA Ops:
  7.2 0.0 all-reduce.8.cloned.1.call-start
  7.2 2.4 convert_reduce_fusion
  9.6 18.7 %all-reduce.1 = (f32[512]{0:T(512)S(1)}, f32[512]{0:T(512)S(1)}) all-reduce(f32[512]{0:T(512)S(1)} %get-tuple-element.3, f32[512]{0:T(512)S(1)} %get-tuple-element.2), channel_id=1, replica_groups=mesh['samp'=8,'blk'=4] {'samp'}, use_global_device_ids=true, to_apply=%region_3.0 | all-reduce | flops 1024 | bytes 8192 | tf_op jit(solution)/shard_map/psum | solution.py:39
  28.3 2.3 multiply_convert_fusion
  30.6 0.0 copy-start.2
  30.6 2.0 fusion.21
  32.7 0.0 copy-done.2
  32.7 0.0 copy-start.3
  32.7 1.0 fusion.16
  33.7 0.0 all-reduce.8.cloned.1.call-update
  33.8 0.0 reduce-scatter.2.cloned.1.call-start
  33.8 0.0 copy-done.3
  33.8 0.1 broadcast_in_dim.2
  33.9 0.1 reshape.58
  34.0 81.3 %all-reduce.8.cloned.1.call-done = (f32[512,64]{0,1:T(8,128)}, f32[512,512]{1,0:T(8,128)}) async-done(((f32[512,64]{0,1:T(8,128)}, f32[512,512]{1,0:T(8,128)}), (f32[512,64]{0,1:T(8,128)}, f32[512,512]{1,0:T(8,128)})) %all-reduce.8.cloned.1.call-update) | async-done | bytes 1179664 | tf_op jit(solution)/shard_map/psum | solution.py:58
  115.2 0.0 copy-start
  115.2 1.5 abs_reduce_fusion
  116.7 0.6 reduce_max.9
  118.0 0.9 broadcast_multiply_fusion
  118.9 0.1 bitcast_divide_fusion
  119.0 0.1 tile.4
  119.1 0.0 copy-done
  119.1 1.3 fusion.6
  120.5 1.6 fusion.7
  122.1 0.0 copy-start.1
  122.1 2.0 fusion.22
  124.1 0.0 reduce-scatter.2.cloned.1.call-update
  124.1 0.0 all-reduce.6.cloned.1.call-start
  124.2 0.0 copy-done.1
  124.2 0.2 convert_reduce_fusion.1
  124.4 29.7 %reduce-scatter.2.cloned.1.call-done = f32[5,16,1536]{2,1,0:T(8,128)} async-done(((f32[5,64,1536]{2,1,0:T(8,128)}), f32[5,16,1536]{2,1,0:T(8,128)}) %reduce-scatter.2.cloned.1.call-update) | async-done | bytes 491536 | tf_op jit(solution)/shard_map/reduce_scatter | solution.py:77
  154.1 1.9 fusion.20
  156.0 9.8 %all_gather.3 = bf16[5,64,1536]{2,1,0:T(8,128)(2,1)S(1)} all-gather(bf16[5,16,1536]{2,1,0:T(8,128)(2,1)S(1)} %get-tuple-element.13), channel_id=1, replica_groups=mesh['samp'=8,'blk'=4] {'blk'}, dimensions={1}, use_global_device_ids=true | all-gather | bytes 1228800 | tf_op jit(solution)/shard_map/all_gather | solution.py:80
  165.8 0.3 multiply_reduce_fusion.1
  166.1 0.1 reduce_sum.62
  166.1 17.6 %all-reduce = (f32[128]{0:T(128)S(1)}, f32[128]{0:T(128)S(1)}, f32[320]{0:T(512)S(1)}) all-reduce(f32[128]{0:T(128)S(1)} %get-tuple-element.5, f32[128]{0:T(128)S(1)} %get-tuple-element.4, f32[320]{0:T(512)S(1)} %reduce_sum.62), channel_id=1, replica_groups=mesh['samp'=8,'blk'=4] {'samp'}, use_global_device_ids=true, to_apply=%region_12.0 | all-reduce | flops 576 | bytes 4608 | tf_op jit(solution)/shard_map/psum | solution.py:39
  183.7 1.1 fusion.11
  184.8 0.0 all-reduce.6.cloned.1.call-update
  184.9 67.8 %all-reduce.6.cloned.1.call-done = f32[320,128]{1,0:T(8,128)} async-done(((f32[320,128]{1,0:T(8,128)}), f32[320,128]{1,0:T(8,128)}) %all-reduce.6.cloned.1.call-update) | async-done | bytes 163856 | tf_op jit(solution)/shard_map/psum | solution.py:84
  252.7 1.7 broadcast_divide_fusion
  (6 shorter events, 0.1 us)
Async XLA Ops:
  7.2 108.1 %all-reduce.8.cloned.1.call-start = ((), (), s32[]{:S(2)}) async-start(), calls=%async_computation.3 | async-start | bytes 2359296 | tf_op jit(solution)/shard_map/psum | solution.py:58
  30.6 2.1 copy-start.2
  32.7 1.1 copy-start.3
  33.8 120.4 %reduce-scatter.2.cloned.1.call-start = ((), (), s32[]{:S(2)}) async-start(), calls=%async_computation.1 | async-start | bytes 2457600 | tf_op jit(solution)/shard_map/reduce_scatter | solution.py:77
  115.2 3.9 %copy-start = (f32[512,512]{1,0:T(8,128)S(1)}, f32[512,512]{1,0:T(8,128)}, u32[]{:S(2)}) copy-start(f32[512,512]{1,0:T(8,128)} %get-tuple-element.12) | copy-start | bytes 3145732
  122.1 2.1 copy-start.1
  124.1 128.5 %all-reduce.6.cloned.1.call-start = ((), (), s32[]{:S(2)}) async-start(), calls=%async_computation.2 | async-start | bytes 327680 | tf_op jit(solution)/shard_map/psum | solution.py:84
Sparse Core Ops, SparseCore 0:
  33.9 81.3 all-reduce.7
  124.3 29.8 reduce-scatter.1
  185.0 67.6 all-reduce.5
where the time goes:
time: 264 us; the launch traced here: 261 us
  waiting for transfers between devices  179 us (68%)
  blocking collectives  46.1 us (17%)
  between operations  14.5 us (5%)
  other arithmetic  11.9 us (5%)
  matrix products  9.15 us (3%)
    psum x1, waiting for transfers between devices, shards(): gram_full, cross_full = lax.psum((gram, cross), 'samp')  81.3 us
    psum x1, waiting for transfers between devices, shards(): lax.psum((raw_part, jnp.sum(res_float * res_float, axis=1)), 'samp')  67.8 us
    psum x2, blocking collectives, shards(): lax.psum((jnp.sum(block_codes, axis=0), jnp.sum(block_codes * block_codes...  36.3 us
    reduce_scatter x1, waiting for transfers between devices, shards(): pred_part = lax.psum_scatter(pred, 'blk', scatter_dimension=1, tiled=True)  29.7 us
    all_gather x1, blocking collectives, shards(): lax.all_gather(residual.astype(jnp.bfloat16), 'blk', axis=1, tiled=True)  9.78 us
  transfers between devices with their start and end apart: 3, of which 3 were waited for; matrix products, arithmetic and copies ran while one was open for 0% of the time, Pallas kernels for 0%

commit v1 on v0

v1 whole, which is shorter than its diff:
```python
import functools

import jax
import jax.numpy as jnp
from jax import lax
from jax.experimental import pallas as pl
from jax.experimental.pallas import tpu as pltpu
from jax.sharding import PartitionSpec as P

RIDGE = 5
CHEB = 3
LANES = 128
F32 = jnp.float32
BF16 = jnp.bfloat16
MESH = pl.DeviceIdType.MESH


def up(value, unit):
    return -(-value // unit) * unit


def coefficients(lam, bound):
    centre = lam + bound / 2.0
    half = bound / 2.0
    sig = centre / half
    factor = 1.0 / sig
    zero = jnp.zeros_like(centre)
    direction = [1.0 / centre] + [zero] * (CHEB - 1)
    remain = [zero + 1.0] + [zero] * (CHEB - 1)
    iterate = [zero] * CHEB
    for sweep in range(CHEB):
        iterate = [a + b for a, b in zip(iterate, direction)]
        if sweep + 1 < CHEB:
            applied = [lam * direction[0]] + [
                lam * direction[i] + direction[i - 1] for i in range(1, CHEB)
            ]
            remain = [a - b for a, b in zip(remain, applied)]
            following = 1.0 / (2.0 * sig - factor)
            direction = [
                following * factor * a + 2.0 * following / half * b
                for a, b in zip(direction, remain)
            ]
            factor = following
    return iterate


def kernel(
    ns, nb, share, count, chunk,
    shrink_ref, dos_ref, new_ref, traits_ref,
    residual_ref, scores_ref,
    x_ref, fresh_ref, st_src, st_dst, part, rs_dst, gath, gram_ref, w_ref,
    core_src, keep, core_dst, y_src, y_dst, rw_src, rw_dst, fin_src, fin_dst,
    st_s, st_r, rs_s, rs_r, ag_s, ag_r, fr_s, fr_r, core_s, core_r, y_s, y_r,
    rw_s, rw_r, fin_s, fin_r,
):
    s = lax.axis_index("samp")
    b = lax.axis_index("blk")
    ny = nb // 2
    core = lax.rem(b, 2)
    y = b // 2
    rows, vb = dos_ref.shape
    nc = new_ref.shape[1]
    nt = traits_ref.shape[0]
    vblocks = vb // LANES
    own = RIDGE * share
    q = nb * own // ns
    k = ns // nb
    total = ns * nb
    me = s * nb + b

    barrier = pltpu.get_barrier_semaphore()

    def greet(i, carry):
        other = lax.rem(me + i, total)
        pl.semaphore_signal(
            barrier, inc=1, device_id=(other // nb, lax.rem(other, nb)), device_id_type=MESH
        )
        return carry

    lax.fori_loop(1, total, greet, 0)

    sends = []

    def send(src, dst, ssem, rsem, device):
        copy = pltpu.make_async_remote_copy(
            src_ref=src, dst_ref=dst, send_sem=ssem, recv_sem=rsem,
            device_id=device, device_id_type=MESH,
        )
        copy.start()
        sends.append(copy)
        return copy

    st_src[...] = jnp.zeros_like(st_src)
    codes = dos_ref[...].astype(F32)
    st_src[0:1, :vb] = jnp.sum(codes, axis=0, keepdims=True)
    st_src[1:2, :vb] = jnp.sum(codes * codes, axis=0, keepdims=True)
    codes = new_ref[...].astype(F32)
    st_src[0:1, vb:] = jnp.sum(codes, axis=0, keepdims=True)
    st_src[1:2, vb:] = jnp.sum(codes * codes, axis=0, keepdims=True)

    pl.semaphore_wait(barrier, total - 1)
    copies = []
    for o in range(1, ns):
        copies.append(
            send(st_src, st_dst.at[o], st_s.at[o], st_r.at[o], (lax.rem(s + o, ns), b))
        )
    stat = st_src[...]
    for o in range(1, ns):
        copies[o - 1].wait_recv()
        stat = stat + st_dst[o]
    mean = stat[0:1] / count
    inv = 1.0 / jnp.sqrt(stat[1:2] / count - mean * mean + 1e-05)
    fresh_ref[b] = ((new_ref[...].astype(F32) - mean[:, vb:]) * inv[:, vb:]).astype(BF16)
    fresh_copies = []
    for o in range(1, nb):
        fresh_copies.append(
            send(fresh_ref.at[b], fresh_ref.at[b], fr_s.at[o], fr_r.at[o], (s, lax.rem(b + o, nb)))
        )
    x_ref[...] = ((dos_ref[...].astype(F32) - mean[:, :vb]) * inv[:, :vb]).astype(BF16)

    x = x_ref[...]
    at = 0
    for i in range(vblocks):
        line = lax.dot_general(
            x[:, i * LANES : (i + 1) * LANES], x[:, i * LANES :],
            (((0,), (0,)), ((), ())), preferred_element_type=F32,
        ).astype(BF16)
        for j in range(vblocks - i):
            part[at : at + LANES, :] = line[:, j * LANES : (j + 1) * LANES]
            at += LANES
    cross = jnp.dot(
        traits_ref[...].astype(BF16), x, preferred_element_type=F32
    ).astype(BF16)
    for j in range(vblocks):
        part[at : at + nt, :] = cross[:, j * LANES : (j + 1) * LANES]
        at += nt
    if at < ns * chunk:
        part[at:, :] = jnp.zeros((ns * chunk - at, LANES), BF16)

    def piece(index):
        return pl.ds(pl.multiple_of(index * chunk, 16), chunk)

    copies = []
    for o in range(1, ns):
        to = lax.rem(s + o, ns)
        copies.append(
            send(part.at[piece(to)], rs_dst.at[o], rs_s.at[o], rs_r.at[o], (to, b))
        )
    summed = part[piece(s), :].astype(F32)
    for o in range(1, ns):
        copies[o - 1].wait_recv()
        summed = summed + rs_dst[o].astype(F32)
    gath[piece(s), :] = summed.astype(BF16)
    copies = []
    for o in range(1, ns):
        to = lax.rem(s + o, ns)
        copies.append(
            send(gath.at[piece(s)], gath.at[piece(s)], ag_s.at[o], ag_r.at[o], (to, b))
        )
    for o in range(1, ns):
        source = lax.rem(s - o + ns, ns)
        pltpu.make_async_remote_copy(
            src_ref=gath.at[piece(source)], dst_ref=gath.at[piece(source)],
            send_sem=ag_s.at[o], recv_sem=ag_r.at[o],
            device_id=(source, b), device_id_type=MESH,
        ).wait_recv()

    at = 0
    for i in range(vblocks):
        for j in range(i, vblocks):
            block = gath[at : at + LANES, :].astype(F32)
            at += LANES
            gram_ref[i * LANES : (i + 1) * LANES, j * LANES : (j + 1) * LANES] = block.astype(BF16)
            if j > i:
                gram_ref[j * LANES : (j + 1) * LANES, i * LANES : (i + 1) * LANES] = block.T.astype(BF16)
    cross = jnp.concatenate(
        [gath[at + j * nt : at + (j + 1) * nt, :] for j in range(vblocks)], axis=1
    )
    gram = gram_ref[...]
    bound = jnp.max(
        jnp.sum(jnp.abs(gram.astype(F32)), axis=0, keepdims=True), axis=1, keepdims=True
    ) / count
    bound = jnp.broadcast_to(bound, (1, vb))

    def apply(value):
        high = value.astype(BF16)
        low = (value - high.astype(F32)).astype(BF16)
        return (
            jnp.dot(high, gram, preferred_element_type=F32)
            + jnp.dot(low, gram, preferred_element_type=F32)
        ) / count

    powers = [cross.astype(F32) / count]
    for _ in range(CHEB - 1):
        powers.append(apply(powers[-1]))
    for r in range(RIDGE):
        coefs = coefficients(jnp.full((1, vb), shrink_ref[r], F32), bound)
        weight = coefs[0] * powers[0]
        for c, v in zip(coefs[1:], powers[1:]):
            weight = weight + c * v
        weight = weight.astype(BF16)
        for d in range(nb):
            w_ref[d, r * share : (r + 1) * share, :] = weight[d * share : (d + 1) * share, :]

    for d in range(nb):
        pred = lax.dot_general(
            w_ref[d], x, (((1,), (1,)), ((), ())), preferred_element_type=F32
        )

        @pl.when(core == d % 2)
        def _():
            keep[d // 2] = pred

        @pl.when(core != d % 2)
        def _():
            core_src[d // 2] = pred.astype(BF16)

    copy = send(core_src, core_dst, core_s.at[0], core_r.at[0], (s, 2 * y + 1 - core))
    copy.wait_recv()
    copies = []
    for o in range(1, ny):
        to = lax.rem(y + o, ny)
        y_src[o] = (keep[to] + core_dst[to].astype(F32)).astype(BF16)
        copies.append(
            send(y_src.at[o], y_dst.at[o], y_s.at[o], y_r.at[o], (s, 2 * to + core))
        )
    pred = keep[y] + core_dst[y].astype(F32)
    for o in range(1, ny):
        copies[o - 1].wait_recv()
        pred = pred + y_dst[o].astype(F32)
    mine = traits_ref[pl.ds(pl.multiple_of(b * share, 8), share), :]
    resid = jnp.concatenate([mine] * RIDGE, axis=0) - pred
    for r in range(RIDGE):
        residual_ref[r] = resid[r * share : (r + 1) * share, :]
    res_bf = resid.astype(BF16)
    res_f = res_bf.astype(F32)
    squares = jnp.zeros((own, LANES), F32)
    for j in range(rows // LANES):
        v = res_f[:, j * LANES : (j + 1) * LANES]
        squares = squares + v * v
    for copy in fresh_copies:
        copy.wait_recv()
    for d in range(nb):
        raw = jnp.dot(res_bf, fresh_ref[d], preferred_element_type=F32)
        for i in range(k):
            rw_src[d * k + i, 0] = raw[i * q : (i + 1) * q, :]
            rw_src[d * k + i, 1] = squares[i * q : (i + 1) * q, :]
    copies = []
    for o in range(1, ns):
        to = lax.rem(s + o, ns)
        copies.append(send(rw_src.at[to], rw_dst.at[o], rw_s.at[o], rw_r.at[o], (to, b)))
    raw = rw_src[s, 0]
    squares = rw_src[s, 1]
    for o in range(1, ns):
        copies[o - 1].wait_recv()
        raw = raw + rw_dst[o, 0]
        squares = squares + rw_dst[o, 1]
    norm = jnp.sum(squares, axis=1, keepdims=True)
    fin_src[...] = raw / jnp.sqrt(count * (norm / count + 1e-05))

    goal = s // k
    slot = lax.rem(s, k)
    for o in range(ns):
        copy = pltpu.make_async_remote_copy(
            src_ref=fin_src, dst_ref=fin_dst.at[b, slot],
            send_sem=fin_s.at[o], recv_sem=fin_r.at[slot * nb + b],
            device_id=(lax.rem(s + o, ns), goal), device_id_type=MESH,
        )
        if o == 0:
            @pl.when(goal != b)
            def _():
                copy.start()

            @pl.when(goal == b)
            def _():
                fin_dst[b, slot] = fin_src[...]
        else:
            copy.start()
            sends.append(copy)
    for i in range(k):
        for d in range(nb):
            source = b * k + i

            @pl.when(jnp.logical_or(source != s, b != d))
            def _():
                pltpu.make_async_remote_copy(
                    src_ref=fin_src, dst_ref=fin_dst.at[d, i],
                    send_sem=fin_s.at[0], recv_sem=fin_r.at[i * nb + d],
                    device_id=(source, d), device_id_type=MESH,
                ).wait_recv()

    for d in range(nb):
        block = jnp.concatenate([fin_dst[d, i] for i in range(k)], axis=0)
        for r in range(RIDGE):
            scores_ref[r, d * share : (d + 1) * share, :] = block[r * share : (r + 1) * share, :]

    for copy in sends:
        copy.wait_send()

    @pl.when(goal != b)
    def _():
        pltpu.make_async_remote_copy(
            src_ref=fin_src, dst_ref=fin_dst.at[b, slot],
            send_sem=fin_s.at[0], recv_sem=fin_r.at[slot * nb + b],
            device_id=(s, goal), device_id_type=MESH,
        ).wait_send()


def shards(ns, nb, dosages, new_dosages, traits, shrink):
    rows, vb = dosages.shape
    nc = new_dosages.shape[1]
    real = traits.shape[0] // nb
    share = up(real, 16)
    if share != real:
        traits = jnp.pad(
            traits.reshape(nb, real, rows), ((0, 0), (0, share - real), (0, 0))
        ).reshape(nb * share, rows)
    nt = nb * share
    vblocks = vb // LANES
    chunk = up(-(-(vblocks * (vblocks + 1) // 2 * LANES + vblocks * nt) // ns), 16)
    own = RIDGE * share
    ny = nb // 2
    k = ns // nb
    q = own // k
    count = float(rows * ns)
    dma = pltpu.SemaphoreType.DMA
    vmem = pl.BlockSpec(memory_space=pltpu.VMEM)
    residual, scores = pl.pallas_call(
        functools.partial(kernel, ns, nb, share, count, chunk),
        out_shape=(
            jax.ShapeDtypeStruct((RIDGE, share, rows), F32),
            jax.ShapeDtypeStruct((RIDGE, nt, nc), F32),
        ),
        in_specs=[pl.BlockSpec(memory_space=pltpu.SMEM), vmem, vmem, vmem],
        out_specs=(vmem, vmem),
        scratch_shapes=[
            pltpu.VMEM((rows, vb), BF16),
            pltpu.VMEM((nb, rows, nc), BF16),
            pltpu.VMEM((8, vb + nc), F32),
            pltpu.VMEM((ns, 8, vb + nc), F32),
            pltpu.VMEM((ns * chunk, LANES), BF16),
            pltpu.VMEM((ns, chunk, LANES), BF16),
            pltpu.VMEM((ns * chunk, LANES), BF16),
            pltpu.VMEM((vb, vb), BF16),
            pltpu.VMEM((nb, own, vb), BF16),
            pltpu.VMEM((ny, own, rows), BF16),
            pltpu.VMEM((ny, own, rows), F32),
            pltpu.VMEM((ny, own, rows), BF16),
            pltpu.VMEM((ny, own, rows), BF16),
            pltpu.VMEM((ny, own, rows), BF16),
            pltpu.VMEM((ns, 2, q, nc), F32),
            pltpu.VMEM((ns, 2, q, nc), F32),
            pltpu.VMEM((q, nc), F32),
            pltpu.VMEM((nb, k, q, nc), F32),
            dma((ns,)), dma((ns,)), dma((ns,)), dma((ns,)), dma((ns,)), dma((ns,)),
            dma((nb,)), dma((nb,)), dma((1,)), dma((1,)), dma((ny,)), dma((ny,)),
            dma((ns,)), dma((ns,)), dma((ns,)), dma((ns,)),
        ],
        compiler_params=pltpu.CompilerParams(
            collective_id=0, has_side_effects=True, vmem_limit_bytes=56 * 1024 * 1024
        ),
    )(shrink, dosages, new_dosages, traits)
    if share != real:
        residual = residual[:, :real]
        scores = scores.reshape(RIDGE, nb, share, nc)[:, :, :real].reshape(RIDGE, nb * real, nc)
    return residual, scores


def solution(mesh):
    placed = (P("samp", "blk"), P("samp", "blk"), P(None, "samp"), P())
    return jax.shard_map(
        functools.partial(shards, mesh.shape["samp"], mesh.shape["blk"]),
        mesh=mesh,
        in_specs=placed,
        out_specs=(P(None, "blk", "samp"), P(None, None, "blk")),
        check_vma=False,
    )
```

time: 264 us -> 65.9 us (0.25)
  waiting for transfers between devices: 179 us -> 0 us
  Pallas kernels: 0 us -> 61.2 us
  blocking collectives: 46.1 us -> 0 us
  between operations: 14.5 us -> 0.64 us
  other arithmetic: 11.9 us -> 0 us
  matrix products: 9.15 us -> 0 us
  local copies, waits for them, and re-layouts: 0.32 us -> 3.44 us
    psum x2 -> x0, waiting for transfers between devices: 149 us -> none  [the longest x1 81.3 us: shards(): gram_full, cross_full = lax.psum((gram, cross), 'samp')]
    pallas_call x0 -> x1, Pallas kernels: none -> 61.2 us  [shards(): pl.pallas_call(functools.partial(kernel, ns, nb, share, count, chunk), ou...]
    psum x2 -> x0, blocking collectives: 36.3 us -> none  [shards(): lax.psum((jnp.sum(block_codes, axis=0), jnp.sum(block_codes * block_codes...]
    reduce_scatter x1 -> x0, waiting for transfers between devices: 29.7 us -> none  [shards(): pred_part = lax.psum_scatter(pred, 'blk', scatter_dimension=1, tiled=True)]
    all_gather x1 -> x0, blocking collectives: 9.78 us -> none  [shards(): lax.all_gather(residual.astype(jnp.bfloat16), 'blk', axis=1, tiled=True)]
    dot_general x6 -> x0, matrix products: 9.15 us -> none  [the longest x2 2.96 us: apply_full(): jnp.dot(gram_full, direction, precision=lax.Precision.HIGHEST) / count]
    reduce_sum x4 -> x0, other arithmetic: 4.3 us -> none  [the longest x1 2.36 us: shards(): jnp.sum(block_codes, axis=0)]
    convert_element_type x2 -> x0, other arithmetic: 4.2 us -> none  [the longest x1 2.34 us: scaled(): return ((values - column_mean) * inverse).astype(jnp.bfloat16)]
  transfers between devices with their start and end apart: 3 -> 0, of which waited for: 3 -> 0; matrix products, arithmetic and copies ran while one was open for 0% -> 0% of each run, Pallas kernels for 0% -> 0%
where the time goes in v1:
time: 65.9 us; the launch traced here: 65.3 us
  Pallas kernels  61.2 us (93%)
  local copies, waits for them, and re-layouts  3.44 us (5%)
    pallas_call x1, Pallas kernels, shards(): pl.pallas_call(functools.partial(kernel, ns, nb, share, count, chunk), ou...  61.2 us
    unnamed x2, local copies, waits for them, and re-layouts  3.44 us

profile of v1, /device:TPU:1, one launch (start us, length us, event | category | flops | bytes accessed | tf_op | source)
XLA Modules:
  0.0 65.3 jit_solution(14413958501603849275)
XLA Ops:
  0.6 61.2 %shard_map.59 = (f32[5,16,1536]{2,1,0:T(8,128)}, f32[5,64,128]{2,1,0:T(8,128)}) custom-call(f32[5]{0:T(128)} %shrink_ref.1, s32[1536,512]{1,0:T(8,128)} %dos_ref.1, s32[1536,128]{1,0:T(8,128)} %new_ref.1, f32[64,1536]{1,0:T(8,128)} %traits_ref.1), custom_call_target="tpu_custom_call" | custom-call | tf_op jit(solution)/shard_map/pallas_call | solution.py:328
  61.8 1.8 %copy.8 = f32[5,16,1536]{2,1,0:T(8,128)} copy(f32[5,16,1536]{2,1,0:T(8,128)} %get-tuple-element.4) | data formatting | bytes 983040
  63.7 1.6 %copy.9 = f32[5,64,128]{2,1,0:T(8,128)} copy(f32[5,64,128]{2,1,0:T(8,128)} %get-tuple-element.5) | data formatting | bytes 327680

commit v2 on v1

--- a/solution.py
+++ b/solution.py
@@ -51,7 +51,7 @@
     x_ref, fresh_ref, st_src, st_dst, part, rs_dst, gath, gram_ref, w_ref,
     core_src, keep, core_dst, y_src, y_dst, rw_src, rw_dst, fin_src, fin_dst,
     st_s, st_r, rs_s, rs_r, ag_s, ag_r, fr_s, fr_r, core_s, core_r, y_s, y_r,
-    rw_s, rw_r, fin_s, fin_r,
+    rw_s, rw_r, fin_s, fin_r, tw_s, tw_r, tg_s, tg_r, tw_dst, rs_src, norm_ref,
 ):
     s = lax.axis_index("samp")
     b = lax.axis_index("blk")
@@ -65,19 +65,13 @@
     own = RIDGE * share
     q = nb * own // ns
     k = ns // nb
-    total = ns * nb
-    me = s * nb + b
 
     barrier = pltpu.get_barrier_semaphore()
 
-    def greet(i, carry):
-        other = lax.rem(me + i, total)
-        pl.semaphore_signal(
-            barrier, inc=1, device_id=(other // nb, lax.rem(other, nb)), device_id_type=MESH
-        )
-        return carry
-
-    lax.fori_loop(1, total, greet, 0)
+    others = [(lax.rem(s + o, ns), b) for o in range(1, ns)]
+    others += [(s, lax.rem(b + o, nb)) for o in range(1, nb)]
+    for other in others:
+        pl.semaphore_signal(barrier, inc=1, device_id=other, device_id_type=MESH)
 
     sends = []
 
@@ -90,7 +84,6 @@
         sends.append(copy)
         return copy
 
-    st_src[...] = jnp.zeros_like(st_src)
     codes = dos_ref[...].astype(F32)
     st_src[0:1, :vb] = jnp.sum(codes, axis=0, keepdims=True)
     st_src[1:2, :vb] = jnp.sum(codes * codes, axis=0, keepdims=True)
@@ -98,7 +91,7 @@
     st_src[0:1, vb:] = jnp.sum(codes, axis=0, keepdims=True)
     st_src[1:2, vb:] = jnp.sum(codes * codes, axis=0, keepdims=True)
 
-    pl.semaphore_wait(barrier, total - 1)
+    pl.semaphore_wait(barrier, len(others))
     copies = []
     for o in range(1, ns):
         copies.append(
@@ -140,29 +133,48 @@
     def piece(index):
         return pl.ds(pl.multiple_of(index * chunk, 16), chunk)
 
+    np = ns // 2
+    lane = lax.rem(s, 2)
+    pair = s // 2
+    twin = s + 1 - 2 * lane
     copies = []
-    for o in range(1, ns):
-        to = lax.rem(s + o, ns)
+    for o in list(range(1, np)) + [0]:
+        to = 2 * lax.rem(pair + o, np) + 1 - lane
         copies.append(
-            send(part.at[piece(to)], rs_dst.at[o], rs_s.at[o], rs_r.at[o], (to, b))
-        )
-    summed = part[piece(s), :].astype(F32)
-    for o in range(1, ns):
+            send(part.at[piece(to)], tw_dst.at[o], tw_s.at[o], tw_r.at[o], (twin, b))
+        )
+    arrivals = []
+    for o in range(1, np):
+        to = 2 * lax.rem(pair + o, np) + lane
         copies[o - 1].wait_recv()
+        rs_src[o] = (part[piece(to), :].astype(F32) + tw_dst[o].astype(F32)).astype(BF16)
+        arrivals.append(
+            send(rs_src.at[o], rs_dst.at[o], rs_s.at[o], rs_r.at[o], (to, b))
+        )
+    copies[np - 1].wait_recv()
+    summed = part[piece(s), :].astype(F32) + tw_dst[0].astype(F32)
+    for o in range(1, np):
+        arrivals[o - 1].wait_recv()
         summed = summed + rs_dst[o].astype(F32)
     gath[piece(s), :] = summed.astype(BF16)
-    copies = []
-    for o in range(1, ns):
-        to = lax.rem(s + o, ns)
-        copies.append(
-            send(gath.at[piece(s)], gath.at[piece(s)], ag_s.at[o], ag_r.at[o], (to, b))
-        )
-    for o in range(1, ns):
-        source = lax.rem(s - o + ns, ns)
+    for o in range(1, np):
+        to = 2 * lax.rem(pair + o, np) + lane
+        send(gath.at[piece(s)], gath.at[piece(s)], ag_s.at[o], ag_r.at[o], (to, b))
+    send(gath.at[piece(s)], gath.at[piece(s)], tg_s.at[0], tg_r.at[0], (twin, b))
+    for o in range(1, np):
+        source = 2 * lax.rem(pair - o + np, np) + lane
         pltpu.make_async_remote_copy(
             src_ref=gath.at[piece(source)], dst_ref=gath.at[piece(source)],
             send_sem=ag_s.at[o], recv_sem=ag_r.at[o],
             device_id=(source, b), device_id_type=MESH,
+        ).wait_recv()
+        send(gath.at[piece(source)], gath.at[piece(source)], tg_s.at[o], tg_r.at[o], (twin, b))
+    for o in range(np):
+        source = 2 * lax.rem(pair - o + np, np) + 1 - lane
+        pltpu.make_async_remote_copy(
+            src_ref=gath.at[piece(source)], dst_ref=gath.at[piece(source)],
+            send_sem=tg_s.at[o], recv_sem=tg_r.at[o],
+            device_id=(twin, b), device_id_type=MESH,
         ).wait_recv()
 
     at = 0
@@ -238,28 +250,33 @@
     for j in range(rows // LANES):
         v = res_f[:, j * LANES : (j + 1) * LANES]
         squares = squares + v * v
+    wide = jnp.concatenate([squares, jnp.zeros((LANES - own, LANES), F32)], axis=0)
+    sums = jnp.broadcast_to(jnp.sum(wide.T, axis=0, keepdims=True), (8, LANES))
     for copy in fresh_copies:
         copy.wait_recv()
     for d in range(nb):
         raw = jnp.dot(res_bf, fresh_ref[d], preferred_element_type=F32)
         for i in range(k):
-            rw_src[d * k + i, 0] = raw[i * q : (i + 1) * q, :]
-            rw_src[d * k + i, 1] = squares[i * q : (i + 1) * q, :]
+            rw_src[d * k + i, :q, :] = raw[i * q : (i + 1) * q, :]
+            rw_src[d * k + i, q:, :] = sums
     copies = []
     for o in range(1, ns):
         to = lax.rem(s + o, ns)
         copies.append(send(rw_src.at[to], rw_dst.at[o], rw_s.at[o], rw_r.at[o], (to, b)))
-    raw = rw_src[s, 0]
-    squares = rw_src[s, 1]
+    raw = rw_src[s]
     for o in range(1, ns):
         copies[o - 1].wait_recv()
-        raw = raw + rw_dst[o, 0]
-        squares = squares + rw_dst[o, 1]
-    norm = jnp.sum(squares, axis=1, keepdims=True)
-    fin_src[...] = raw / jnp.sqrt(count * (norm / count + 1e-05))
+        raw = raw + rw_dst[o]
 
     goal = s // k
     slot = lax.rem(s, k)
+    norm_ref[...] = raw[q:, :].T[:own, :]
+    norm = norm_ref[pl.ds(pl.multiple_of(slot * q, 8), q), 0:1]
+    score = raw[:q, :] / jnp.sqrt(count * (norm / count + 1e-05))
+    extra = up(q, 16) - q
+    if extra:
+        score = jnp.concatenate([score, jnp.zeros((extra, nc), F32)], axis=0)
+    fin_src[...] = score.astype(BF16)
     for o in range(ns):
         copy = pltpu.make_async_remote_copy(
             src_ref=fin_src, dst_ref=fin_dst.at[b, slot],
@@ -290,7 +307,7 @@
                 ).wait_recv()
 
     for d in range(nb):
-        block = jnp.concatenate([fin_dst[d, i] for i in range(k)], axis=0)
+        block = jnp.concatenate([fin_dst[d, i].astype(F32)[:q] for i in range(k)], axis=0)
         for r in range(RIDGE):
             scores_ref[r, d * share : (d + 1) * share, :] = block[r * share : (r + 1) * share, :]
 
@@ -336,10 +353,10 @@
         scratch_shapes=[
             pltpu.VMEM((rows, vb), BF16),
             pltpu.VMEM((nb, rows, nc), BF16),
-            pltpu.VMEM((8, vb + nc), F32),
-            pltpu.VMEM((ns, 8, vb + nc), F32),
+            pltpu.VMEM((2, vb + nc), F32),
+            pltpu.VMEM((ns, 2, vb + nc), F32),
             pltpu.VMEM((ns * chunk, LANES), BF16),
-            pltpu.VMEM((ns, chunk, LANES), BF16),
+            pltpu.VMEM((ns // 2, chunk, LANES), BF16),
             pltpu.VMEM((ns * chunk, LANES), BF16),
             pltpu.VMEM((vb, vb), BF16),
             pltpu.VMEM((nb, own, vb), BF16),
@@ -348,13 +365,17 @@
             pltpu.VMEM((ny, own, rows), BF16),
             pltpu.VMEM((ny, own, rows), BF16),
             pltpu.VMEM((ny, own, rows), BF16),
-            pltpu.VMEM((ns, 2, q, nc), F32),
-            pltpu.VMEM((ns, 2, q, nc), F32),
-            pltpu.VMEM((q, nc), F32),
-            pltpu.VMEM((nb, k, q, nc), F32),
+            pltpu.VMEM((ns, q + 8, nc), F32),
+            pltpu.VMEM((ns, q + 8, nc), F32),
+            pltpu.VMEM((up(q, 16), nc), BF16),
+            pltpu.VMEM((nb, k, up(q, 16), nc), BF16),
             dma((ns,)), dma((ns,)), dma((ns,)), dma((ns,)), dma((ns,)), dma((ns,)),
             dma((nb,)), dma((nb,)), dma((1,)), dma((1,)), dma((ny,)), dma((ny,)),
             dma((ns,)), dma((ns,)), dma((ns,)), dma((ns,)),
+            dma((ns // 2,)), dma((ns // 2,)), dma((ns // 2,)), dma((ns // 2,)),
+            pltpu.VMEM((ns // 2, chunk, LANES), BF16),
+            pltpu.VMEM((ns // 2, chunk, LANES), BF16),
+            pltpu.VMEM((own, 8), F32),
         ],
         compiler_params=pltpu.CompilerParams(
             collective_id=0, has_side_effects=True, vmem_limit_bytes=56 * 1024 * 1024

time: 65.9 us -> 58.2 us (0.88)
  Pallas kernels: 61.2 us -> 53.9 us
    pallas_call x1, Pallas kernels: 61.2 us -> 53.9 us  [shards(): pl.pallas_call(functools.partial(kernel, ns, nb, share, count, chunk), ou...]
where the time goes in v2:
time: 58.2 us; the launch traced here: 58 us
  Pallas kernels  53.9 us (93%)
  local copies, waits for them, and re-layouts  3.44 us (6%)
  between operations  0.64 us (1%)
    pallas_call x1, Pallas kernels, shards(): pl.pallas_call(functools.partial(kernel, ns, nb, share, count, chunk), ou...  53.9 us
    unnamed x2, local copies, waits for them, and re-layouts  3.44 us

profile of v2, /device:TPU:1, one launch (start us, length us, event | category | flops | bytes accessed | tf_op | source)
XLA Modules:
  0.0 58.0 jit_solution(12240263001663184599)
XLA Ops:
  0.6 53.9 %shard_map.59 = (f32[5,16,1536]{2,1,0:T(8,128)}, f32[5,64,128]{2,1,0:T(8,128)}) custom-call(f32[5]{0:T(128)} %shrink_ref.1, s32[1536,512]{1,0:T(8,128)} %dos_ref.1, s32[1536,128]{1,0:T(8,128)} %new_ref.1, f32[64,1536]{1,0:T(8,128)} %traits_ref.1), custom_call_target="tpu_custom_call" | custom-call | tf_op jit(solution)/shard_map/pallas_call | solution.py:345
  54.6 1.8 %copy.8 = f32[5,16,1536]{2,1,0:T(8,128)} copy(f32[5,16,1536]{2,1,0:T(8,128)} %get-tuple-element.4) | data formatting | bytes 983040
  56.4 1.6 %copy.9 = f32[5,64,128]{2,1,0:T(8,128)} copy(f32[5,64,128]{2,1,0:T(8,128)} %get-tuple-element.5) | data formatting | bytes 327680

commit v3 on v2

--- a/solution.py
+++ b/solution.py
@@ -49,9 +49,9 @@
     shrink_ref, dos_ref, new_ref, traits_ref,
     residual_ref, scores_ref,
     x_ref, fresh_ref, st_src, st_dst, part, rs_dst, gath, gram_ref, w_ref,
-    core_src, keep, core_dst, y_src, y_dst, rw_src, rw_dst, fin_src, fin_dst,
+    core_src, core_dst, y_src, y_dst, rw_src, rw_dst, fin_src, fin_dst,
     st_s, st_r, rs_s, rs_r, ag_s, ag_r, fr_s, fr_r, core_s, core_r, y_s, y_r,
-    rw_s, rw_r, fin_s, fin_r, tw_s, tw_r, tg_s, tg_r, tw_dst, rs_src, norm_ref,
+    rw_s, rw_r, fin_s, fin_r, tw_s, tw_r, tg_s, tg_r, tw_dst, rs_src, norm_ref, st_sum, fc_s, fc_r,
 ):
     s = lax.axis_index("samp")
     b = lax.axis_index("blk")
@@ -68,8 +68,14 @@
 
     barrier = pltpu.get_barrier_semaphore()
 
-    others = [(lax.rem(s + o, ns), b) for o in range(1, ns)]
-    others += [(s, lax.rem(b + o, nb)) for o in range(1, nb)]
+    np = ns // 2
+    lane = lax.rem(s, 2)
+    pair = s // 2
+    twin = s + 1 - 2 * lane
+    sibling = 2 * y + 1 - core
+    others = [(twin, b), (s, sibling)]
+    others += [(2 * lax.rem(pair + o, np) + lane, b) for o in range(1, np)]
+    others += [(s, 2 * lax.rem(y + o, ny) + core) for o in range(1, ny)]
     for other in others:
         pl.semaphore_signal(barrier, inc=1, device_id=other, device_id_type=MESH)
 
@@ -92,23 +98,23 @@
     st_src[1:2, vb:] = jnp.sum(codes * codes, axis=0, keepdims=True)
 
     pl.semaphore_wait(barrier, len(others))
+    send(st_src, st_dst.at[0], st_s.at[0], st_r.at[0], (twin, b)).wait_recv()
+    st_sum[...] = st_src[...] + st_dst[0]
     copies = []
-    for o in range(1, ns):
-        copies.append(
-            send(st_src, st_dst.at[o], st_s.at[o], st_r.at[o], (lax.rem(s + o, ns), b))
-        )
-    stat = st_src[...]
-    for o in range(1, ns):
-        copies[o - 1].wait_recv()
+    for o in range(1, np):
+        to = 2 * lax.rem(pair + o, np) + lane
+        copies.append(send(st_sum, st_dst.at[o], st_s.at[o], st_r.at[o], (to, b)))
+    stat = st_sum[...]
+    for copy, o in zip(copies, range(1, np)):
+        copy.wait_recv()
         stat = stat + st_dst[o]
     mean = stat[0:1] / count
     inv = 1.0 / jnp.sqrt(stat[1:2] / count - mean * mean + 1e-05)
     fresh_ref[b] = ((new_ref[...].astype(F32) - mean[:, vb:]) * inv[:, vb:]).astype(BF16)
-    fresh_copies = []
-    for o in range(1, nb):
-        fresh_copies.append(
-            send(fresh_ref.at[b], fresh_ref.at[b], fr_s.at[o], fr_r.at[o], (s, lax.rem(b + o, nb)))
-        )
+    for o in range(1, ny):
+        to = 2 * lax.rem(y + o, ny) + core
+        send(fresh_ref.at[b], fresh_ref.at[b], fr_s.at[o], fr_r.at[o], (s, to))
+    send(fresh_ref.at[b], fresh_ref.at[b], fc_s.at[0], fc_r.at[0], (s, sibling))
     x_ref[...] = ((dos_ref[...].astype(F32) - mean[:, :vb]) * inv[:, :vb]).astype(BF16)
 
     x = x_ref[...]
@@ -133,10 +139,6 @@
     def piece(index):
         return pl.ds(pl.multiple_of(index * chunk, 16), chunk)
 
-    np = ns // 2
-    lane = lax.rem(s, 2)
-    pair = s // 2
-    twin = s + 1 - 2 * lane
     copies = []
     for o in list(range(1, np)) + [0]:
         to = 2 * lax.rem(pair + o, np) + 1 - lane
@@ -214,29 +216,32 @@
         for d in range(nb):
             w_ref[d, r * share : (r + 1) * share, :] = weight[d * share : (d + 1) * share, :]
 
-    for d in range(nb):
-        pred = lax.dot_general(
+    def predict(d):
+        return lax.dot_general(
             w_ref[d], x, (((1,), (1,)), ((), ())), preferred_element_type=F32
         )
 
-        @pl.when(core == d % 2)
-        def _():
-            keep[d // 2] = pred
-
-        @pl.when(core != d % 2)
-        def _():
-            core_src[d // 2] = pred.astype(BF16)
-
-    copy = send(core_src, core_dst, core_s.at[0], core_r.at[0], (s, 2 * y + 1 - core))
-    copy.wait_recv()
     copies = []
+    for o in list(range(1, ny)) + [0]:
+        to = lax.rem(y + o, ny)
+        core_src[o] = predict(2 * to + 1 - core).astype(BF16)
+        copy = send(core_src.at[o], core_dst.at[o], core_s.at[o], core_r.at[o], (s, sibling))
+        pred = predict(2 * to + core)
+        copy.wait_recv()
+        pred = pred + core_dst[o].astype(F32)
+        if o:
+            y_src[o] = pred.astype(BF16)
+            copies.append(
+                send(y_src.at[o], y_dst.at[o], y_s.at[o], y_r.at[o], (s, 2 * to + core))
+            )
     for o in range(1, ny):
-        to = lax.rem(y + o, ny)
-        y_src[o] = (keep[to] + core_dst[to].astype(F32)).astype(BF16)
-        copies.append(
-            send(y_src.at[o], y_dst.at[o], y_s.at[o], y_r.at[o], (s, 2 * to + core))
-        )
-    pred = keep[y] + core_dst[y].astype(F32)
+        source = 2 * lax.rem(y - o + ny, ny) + core
+        pltpu.make_async_remote_copy(
+            src_ref=fresh_ref.at[source], dst_ref=fresh_ref.at[source],
+            send_sem=fr_s.at[o], recv_sem=fr_r.at[o],
+            device_id=(s, source), device_id_type=MESH,
+        ).wait_recv()
+        send(fresh_ref.at[source], fresh_ref.at[source], fc_s.at[o], fc_r.at[o], (s, sibling))
     for o in range(1, ny):
         copies[o - 1].wait_recv()
         pred = pred + y_dst[o].astype(F32)
@@ -252,8 +257,13 @@
         squares = squares + v * v
     wide = jnp.concatenate([squares, jnp.zeros((LANES - own, LANES), F32)], axis=0)
     sums = jnp.broadcast_to(jnp.sum(wide.T, axis=0, keepdims=True), (8, LANES))
-    for copy in fresh_copies:
-        copy.wait_recv()
+    for o in range(ny):
+        source = 2 * lax.rem(y - o + ny, ny) + 1 - core
+        pltpu.make_async_remote_copy(
+            src_ref=fresh_ref.at[source], dst_ref=fresh_ref.at[source],
+            send_sem=fc_s.at[o], recv_sem=fc_r.at[o],
+            device_id=(s, sibling), device_id_type=MESH,
+        ).wait_recv()
     for d in range(nb):
         raw = jnp.dot(res_bf, fresh_ref[d], preferred_element_type=F32)
         for i in range(k):
@@ -361,7 +371,6 @@
             pltpu.VMEM((vb, vb), BF16),
             pltpu.VMEM((nb, own, vb), BF16),
             pltpu.VMEM((ny, own, rows), BF16),
-            pltpu.VMEM((ny, own, rows), F32),
             pltpu.VMEM((ny, own, rows), BF16),
             pltpu.VMEM((ny, own, rows), BF16),
             pltpu.VMEM((ny, own, rows), BF16),
@@ -370,12 +379,14 @@
             pltpu.VMEM((up(q, 16), nc), BF16),
             pltpu.VMEM((nb, k, up(q, 16), nc), BF16),
             dma((ns,)), dma((ns,)), dma((ns,)), dma((ns,)), dma((ns,)), dma((ns,)),
-            dma((nb,)), dma((nb,)), dma((1,)), dma((1,)), dma((ny,)), dma((ny,)),
+            dma((ny,)), dma((ny,)), dma((ny,)), dma((ny,)), dma((ny,)), dma((ny,)),
             dma((ns,)), dma((ns,)), dma((ns,)), dma((ns,)),
             dma((ns // 2,)), dma((ns // 2,)), dma((ns // 2,)), dma((ns // 2,)),
             pltpu.VMEM((ns // 2, chunk, LANES), BF16),
             pltpu.VMEM((ns // 2, chunk, LANES), BF16),
             pltpu.VMEM((own, 8), F32),
+            pltpu.VMEM((2, vb + nc), F32),
+            dma((ny,)), dma((ny,)),
         ],
         compiler_params=pltpu.CompilerParams(
             collective_id=0, has_side_effects=True, vmem_limit_bytes=56 * 1024 * 1024

time: 58.2 us -> 59.9 us (1.029)
  Pallas kernels: 53.9 us -> 55.6 us
    pallas_call x1, Pallas kernels: 53.9 us -> 55.6 us  [shards(): pl.pallas_call(functools.partial(kernel, ns, nb, share, count, chunk), ou...]
where the time goes in v3:
time: 59.9 us; the launch traced here: 59.7 us
  Pallas kernels  55.6 us (93%)
  local copies, waits for them, and re-layouts  3.44 us (6%)
  between operations  0.64 us (1%)
    pallas_call x1, Pallas kernels, shards(): pl.pallas_call(functools.partial(kernel, ns, nb, share, count, chunk), ou...  55.6 us
    unnamed x2, local copies, waits for them, and re-layouts  3.44 us

profile of v3, /device:TPU:1, one launch (start us, length us, event | category | flops | bytes accessed | tf_op | source)
XLA Modules:
  0.0 59.7 jit_solution(4906232554854836197)
XLA Ops:
  0.6 55.6 %shard_map.59 = (f32[5,16,1536]{2,1,0:T(8,128)}, f32[5,64,128]{2,1,0:T(8,128)}) custom-call(f32[5]{0:T(128)} %shrink_ref.1, s32[1536,512]{1,0:T(8,128)} %dos_ref.1, s32[1536,128]{1,0:T(8,128)} %new_ref.1, f32[64,1536]{1,0:T(8,128)} %traits_ref.1), custom_call_target="tpu_custom_call" | custom-call | tf_op jit(solution)/shard_map/pallas_call | solution.py:355
  56.2 1.8 %copy.8 = f32[5,16,1536]{2,1,0:T(8,128)} copy(f32[5,16,1536]{2,1,0:T(8,128)} %get-tuple-element.4) | data formatting | bytes 983040
  58.1 1.6 %copy.9 = f32[5,64,128]{2,1,0:T(8,128)} copy(f32[5,64,128]{2,1,0:T(8,128)} %get-tuple-element.5) | data formatting | bytes 327680

commit v4 on v3

--- a/solution.py
+++ b/solution.py
@@ -51,7 +51,7 @@
     x_ref, fresh_ref, st_src, st_dst, part, rs_dst, gath, gram_ref, w_ref,
     core_src, core_dst, y_src, y_dst, rw_src, rw_dst, fin_src, fin_dst,
     st_s, st_r, rs_s, rs_r, ag_s, ag_r, fr_s, fr_r, core_s, core_r, y_s, y_r,
-    rw_s, rw_r, fin_s, fin_r, tw_s, tw_r, tg_s, tg_r, tw_dst, rs_src, norm_ref, st_sum, fc_s, fc_r,
+    rw_s, rw_r, fin_s, fin_r, tg_s, tg_r, norm_ref, fc_s, fc_r,
 ):
     s = lax.axis_index("samp")
     b = lax.axis_index("blk")
@@ -73,8 +73,7 @@
     pair = s // 2
     twin = s + 1 - 2 * lane
     sibling = 2 * y + 1 - core
-    others = [(twin, b), (s, sibling)]
-    others += [(2 * lax.rem(pair + o, np) + lane, b) for o in range(1, np)]
+    others = [(lax.rem(s + o, ns), b) for o in range(1, ns)] + [(s, sibling)]
     others += [(s, 2 * lax.rem(y + o, ny) + core) for o in range(1, ny)]
     for other in others:
         pl.semaphore_signal(barrier, inc=1, device_id=other, device_id_type=MESH)
@@ -98,15 +97,14 @@
     st_src[1:2, vb:] = jnp.sum(codes * codes, axis=0, keepdims=True)
 
     pl.semaphore_wait(barrier, len(others))
-    send(st_src, st_dst.at[0], st_s.at[0], st_r.at[0], (twin, b)).wait_recv()
-    st_sum[...] = st_src[...] + st_dst[0]
     copies = []
-    for o in range(1, np):
-        to = 2 * lax.rem(pair + o, np) + lane
-        copies.append(send(st_sum, st_dst.at[o], st_s.at[o], st_r.at[o], (to, b)))
-    stat = st_sum[...]
-    for copy, o in zip(copies, range(1, np)):
-        copy.wait_recv()
+    for o in range(1, ns):
+        copies.append(
+            send(st_src, st_dst.at[o], st_s.at[o], st_r.at[o], (lax.rem(s + o, ns), b))
+        )
+    stat = st_src[...]
+    for o in range(1, ns):
+        copies[o - 1].wait_recv()
         stat = stat + st_dst[o]
     mean = stat[0:1] / count
     inv = 1.0 / jnp.sqrt(stat[1:2] / count - mean * mean + 1e-05)
@@ -140,23 +138,14 @@
         return pl.ds(pl.multiple_of(index * chunk, 16), chunk)
 
     copies = []
-    for o in list(range(1, np)) + [0]:
-        to = 2 * lax.rem(pair + o, np) + 1 - lane
+    for o in range(1, ns):
+        to = lax.rem(s + o, ns)
         copies.append(
-            send(part.at[piece(to)], tw_dst.at[o], tw_s.at[o], tw_r.at[o], (twin, b))
-        )
-    arrivals = []
-    for o in range(1, np):
-        to = 2 * lax.rem(pair + o, np) + lane
+            send(part.at[piece(to)], rs_dst.at[o], rs_s.at[o], rs_r.at[o], (to, b))
+        )
+    summed = part[piece(s), :].astype(F32)
+    for o in range(1, ns):
         copies[o - 1].wait_recv()
-        rs_src[o] = (part[piece(to), :].astype(F32) + tw_dst[o].astype(F32)).astype(BF16)
-        arrivals.append(
-            send(rs_src.at[o], rs_dst.at[o], rs_s.at[o], rs_r.at[o], (to, b))
-        )
-    copies[np - 1].wait_recv()
-    summed = part[piece(s), :].astype(F32) + tw_dst[0].astype(F32)
-    for o in range(1, np):
-        arrivals[o - 1].wait_recv()
         summed = summed + rs_dst[o].astype(F32)
     gath[piece(s), :] = summed.astype(BF16)
     for o in range(1, np):
@@ -366,7 +355,7 @@
             pltpu.VMEM((2, vb + nc), F32),
             pltpu.VMEM((ns, 2, vb + nc), F32),
             pltpu.VMEM((ns * chunk, LANES), BF16),
-            pltpu.VMEM((ns // 2, chunk, LANES), BF16),
+            pltpu.VMEM((ns, chunk, LANES), BF16),
             pltpu.VMEM((ns * chunk, LANES), BF16),
             pltpu.VMEM((vb, vb), BF16),
             pltpu.VMEM((nb, own, vb), BF16),
@@ -381,11 +370,8 @@
             dma((ns,)), dma((ns,)), dma((ns,)), dma((ns,)), dma((ns,)), dma((ns,)),
             dma((ny,)), dma((ny,)), dma((ny,)), dma((ny,)), dma((ny,)), dma((ny,)),
             dma((ns,)), dma((ns,)), dma((ns,)), dma((ns,)),
-            dma((ns // 2,)), dma((ns // 2,)), dma((ns // 2,)), dma((ns // 2,)),
-            pltpu.VMEM((ns // 2, chunk, LANES), BF16),
-            pltpu.VMEM((ns // 2, chunk, LANES), BF16),
+            dma((ns // 2,)), dma((ns // 2,)),
             pltpu.VMEM((own, 8), F32),
-            pltpu.VMEM((2, vb + nc), F32),
             dma((ny,)), dma((ny,)),
         ],
         compiler_params=pltpu.CompilerParams(

time: 59.9 us -> 58.7 us (0.980)
  Pallas kernels: 55.6 us -> 54.1 us
    pallas_call x1, Pallas kernels: 55.6 us -> 54.1 us  [shards(): pl.pallas_call(functools.partial(kernel, ns, nb, share, count, chunk), ou...]
where the time goes in v4:
time: 58.7 us; the launch traced here: 58.2 us
  Pallas kernels  54.1 us (92%)
  local copies, waits for them, and re-layouts  3.44 us (6%)
  between operations  0.64 us (1%)
    pallas_call x1, Pallas kernels, shards(): pl.pallas_call(functools.partial(kernel, ns, nb, share, count, chunk), ou...  54.1 us
    unnamed x2, local copies, waits for them, and re-layouts  3.44 us

profile of v4, /device:TPU:1, one launch (start us, length us, event | category | flops | bytes accessed | tf_op | source)
XLA Modules:
  0.0 58.2 jit_solution(11701551249914269719)
XLA Ops:
  0.6 54.1 %shard_map.59 = (f32[5,16,1536]{2,1,0:T(8,128)}, f32[5,64,128]{2,1,0:T(8,128)}) custom-call(f32[5]{0:T(128)} %shrink_ref.1, s32[1536,512]{1,0:T(8,128)} %dos_ref.1, s32[1536,128]{1,0:T(8,128)} %new_ref.1, f32[64,1536]{1,0:T(8,128)} %traits_ref.1), custom_call_target="tpu_custom_call" | custom-call | tf_op jit(solution)/shard_map/pallas_call | solution.py:344
  54.8 1.8 %copy.8 = f32[5,16,1536]{2,1,0:T(8,128)} copy(f32[5,16,1536]{2,1,0:T(8,128)} %get-tuple-element.4) | data formatting | bytes 983040
  56.6 1.6 %copy.9 = f32[5,64,128]{2,1,0:T(8,128)} copy(f32[5,64,128]{2,1,0:T(8,128)} %get-tuple-element.5) | data formatting | bytes 327680
